TPU v7x, 32 devices: a whole 2x2x4 slice. The times are simulated.
32 devices in a mesh: group: 2 (over y), space: 4 (over z), node: 2 (over core), cuts: 2 (over x).
Axes of the slice: x: 2, y: 2, z: 4, core: 2. Of those that a mesh axis runs over, the one named last changes fastest.
Arguments:
- u_start: float32 [32, 64, 512], P(('group', 'space')), parts along dimension 0, may hold values from -2.5 to 2.5
- kappa: float32 [16, 64, 512], P('space'), may hold values from 0.2 to 2
- source: float32 [2, 32, 64, 512], P('cuts', ('group', 'space')), parts along dimension 1, may hold values from -3 to 3
Outputs:
- solution: float32 [4, 4, 16, 64, 512], P(('group', 'cuts'), 'node', 'space'), parts along dimension 0
There are 2 independent parts, one for each index of `group`. A program takes and returns all parts, laid end to end along the dimension named above; an argument that names none is the same for every part. Nothing has to cross between parts.
All inputs are finite; a program needn't handle non-finite values.
Results may differ from a plain program's by a relative error of at most 0.0003.
Values sent between devices are 32-bit elements; how exact they have to be, the bound alone decides.
A program may use at most 64 MiB of HBM per device.

v0:
```python
import jax
import jax.numpy as jnp
import numpy as np
from jax import lax
from jax.experimental import pallas as pl
from jax.experimental.pallas import tpu as pltpu
from jax.sharding import PartitionSpec as P

DT = 0.5
MESH = pl.DeviceIdType.MESH
ROWS = 8


def radau_tables():
    nodes = [0.08858795951270396, 0.4094668644407347, 0.7876594617608471, 1.0]
    table = []
    for row_node in range(4):
        entries = []
        for basis in range(4):
            coeffs = [1.0]
            for other in range(4):
                if other == basis:
                    continue
                scale = 1.0 / (nodes[basis] - nodes[other])
                longer = [0.0] * (len(coeffs) + 1)
                for power in range(len(coeffs)):
                    longer[power + 1] += coeffs[power] * scale
                    longer[power] -= coeffs[power] * nodes[other] * scale
                coeffs = longer
            integral = 0.0
            for power in range(len(coeffs)):
                integral += coeffs[power] * nodes[row_node] ** (power + 1) / (power + 1)
            entries.append(integral)
        table.append(entries)
    return (np.array(table), np.array(nodes) / 4.0)


def kernel(peers, slices, u_ref, k_ref, s_ref, out_ref, kap, u0, its, cond, wts, base, oper, dinv, flx, far, beg,
           in_send, in_recv, halo_send, halo_recv, op_send, op_recv, cut_send, cut_recv, fwd_send, fwd_recv):
    depth, nx, ny = u_ref.shape
    top = depth - 1
    qnp, dnp = radau_tables()
    z, nd, cut = lax.axis_index("space"), lax.axis_index("node"), lax.axis_index("cuts")
    has = (z > 0, z < peers - 1)
    next_cut, prev_cut = cut < slices - 1, cut > 0
    last_core = nd == 1

    def pick(low, high):
        return jnp.where(nd == 0, jnp.float32(low), jnp.float32(high))

    step = [pick(DT * dnp[n], DT * dnp[n + 2]) for n in range(2)]
    whole = [pick(DT * qnp[n].sum(), DT * qnp[n + 2].sum()) for n in range(2)]
    own = [[pick(DT * qnp[n, j], DT * qnp[n + 2, j + 2]) for j in range(2)] for n in range(2)]
    away = [[pick(DT * qnp[n, j + 2], DT * qnp[n + 2, j]) for j in range(2)] for n in range(2)]

    row = lax.broadcasted_iota(jnp.int32, (ROWS, ny), 0)
    lane = lax.broadcasted_iota(jnp.int32, (ROWS, ny), 1)
    chunks = nx // ROWS

    def rows(r):
        return slice(r * ROWS, (r + 1) * ROWS)

    def sides(ref, r):
        here = ref(0, r)
        prev = ref(0, r - 1) if r > 0 else here
        succ = ref(0, r + 1) if r < chunks - 1 else here
        return [
            ref(1, r), ref(-1, r),
            pltpu.roll(jnp.where(row == 0, succ, here), ROWS - 1, 0),
            pltpu.roll(jnp.where(row == ROWS - 1, prev, here), 1, 0),
            pltpu.roll(here, ny - 1, 1),
            pltpu.roll(here, 1, 1),
        ]

    def inside(parts, r):
        out = list(parts)
        if r == chunks - 1:
            out[2] = jnp.where(row == ROWS - 1, 0.0, out[2])
        if r == 0:
            out[3] = jnp.where(row == 0, 0.0, out[3])
        out[4] = jnp.where(lane == ny - 1, 0.0, out[4])
        out[5] = jnp.where(lane == 0, 0.0, out[5])
        return out

    def stencil(n, field, p, r):
        half = cond[n, p + 1, rows(r)]
        near = inside(sides(lambda d, q: cond[n, p + 1 + d, rows(q)], r), r)
        w = [half + c for c in near]
        diag = (w[0] + w[1]) + (w[2] + w[3]) + (w[4] + w[5])
        w = inside(w, r)
        v = sides(lambda d, q: field(p + 1 + d, rows(q)), r)
        flow = (w[0] * v[0] + w[1] * v[1]) + (w[2] * v[2] + w[3] * v[3]) + (w[4] * v[4] + w[5] * v[5])
        return w, diag, flow

    def conduct(n, field, index):
        for r in range(chunks):
            v = field(index, rows(r))
            cond[n, index, rows(r)] = 0.5 * kap[index, rows(r)] * (1.0 + v * v)

    def first(p):
        for r in range(chunks):
            w, diag, flow = stencil(0, lambda i, q: u0[i, q], p, r)
            v = u0[p + 1, rows(r)]
            op = flow - diag * v
            slope = op + s_ref[p, rows(r)]
            for n in range(2):
                inv = 1.0 / (1.0 + step[n] * diag)
                t = inv * (v + whole[n] * slope - step[n] * op)
                base[n, p, rows(r)] = t
                scale = step[n] * inv
                for k in range(6):
                    wts[n, k, p, rows(r)] = w[k] * scale
                its[0, n, p + 1, rows(r)] = t + scale * flow

    def second(n, p):
        s = jnp.where(n == 0, step[0], step[1])
        for r in range(chunks):
            w, diag, flow = stencil(n, lambda i, q: its[2, n, i, q], p, r)
            oper[n, p, rows(r)] = flow - diag * its[2, n, p + 1, rows(r)]
            inv = 1.0 / (1.0 + s * diag)
            scale = s * inv
            for k in range(6):
                wts[n, k, p, rows(r)] = w[k] * scale
            dinv[n, p, rows(r)] = inv
            flx[n, p, rows(r)] = scale * flow

    def combine(p):
        for r in range(chunks):
            q = rows(r)
            a, b, c, d = oper[0, p, q], oper[1, p, q], far[0, p, q], far[1, p, q]
            start, src = beg[p, q], s_ref[p, q]
            for n in range(2):
                t = start + own[n][0] * a + own[n][1] * b + away[n][0] * c + away[n][1] * d + whole[n] * src
                t = dinv[n, p, q] * (t - step[n] * (a, b)[n])
                base[n, p, q] = t
                its[3, n, p + 1, q] = t + flx[n, p, q]

    def jacobi(i, n, p):
        for r in range(chunks):
            v = sides(lambda d, q: its[i, n, p + 1 + d, rows(q)], r)
            w = [wts[n, k, p, rows(r)] for k in range(6)]
            got = base[n, p, rows(r)] + (w[0] * v[0] + w[1] * v[1])
            got = got + ((w[2] * v[2] + w[3] * v[3]) + (w[4] * v[4] + w[5] * v[5]))
            if i == 4:
                out_ref[n, p, rows(r)] = got
            else:
                its[i + 1, n, p + 1, rows(r)] = got

    def halo(i, side, n):
        return pltpu.make_async_remote_copy(
            src_ref=its.at[i, n, 1 if side == 0 else depth],
            dst_ref=its.at[i, n, depth + 1 if side == 0 else 0],
            send_sem=halo_send.at[i, side, n], recv_sem=halo_recv.at[i, side, n],
            device_id={"space": z - 1 if side == 0 else z + 1}, device_id_type=MESH)

    def given(side, which):
        src, dst = ((u_ref, u0), (k_ref, kap))[which]
        return pltpu.make_async_remote_copy(
            src_ref=src.at[0 if side == 0 else top],
            dst_ref=dst.at[depth + 1 if side == 0 else 0],
            send_sem=in_send.at[side, which], recv_sem=in_recv.at[side, which],
            device_id={"space": z - 1 if side == 0 else z + 1}, device_id_type=MESH)

    def terms(n, p):
        return pltpu.make_async_remote_copy(
            src_ref=oper.at[n, p], dst_ref=far.at[n, p],
            send_sem=op_send.at[n, p], recv_sem=op_recv.at[n, p],
            device_id={"node": 1 - nd}, device_id_type=MESH)

    def ending(p):
        return pltpu.make_async_remote_copy(
            src_ref=its.at[2, 1, p + 1], dst_ref=beg.at[p],
            send_sem=cut_send.at[p], recv_sem=cut_recv.at[p],
            device_id={"cuts": cut + 1}, device_id_type=MESH)

    def forward(p):
        return pltpu.make_async_remote_copy(
            src_ref=beg.at[p], dst_ref=beg.at[p],
            send_sem=fwd_send.at[p], recv_sem=fwd_recv.at[p],
            device_id={"node": 1 - nd}, device_id_type=MESH)

    barrier = pltpu.get_barrier_semaphore()

    def greet(**where):
        pl.semaphore_signal(barrier, inc=1, device_id=where, device_id_type=MESH)

    @pl.when(has[0])
    def _():
        greet(space=z - 1)

    @pl.when(has[1])
    def _():
        greet(space=z + 1)

    greet(node=1 - nd)

    @pl.when(jnp.logical_and(last_core, next_cut))
    def _():
        greet(cuts=cut + 1)

    @pl.when(jnp.logical_and(last_core, prev_cut))
    def _():
        greet(cuts=cut - 1)

    def one(flag):
        return jnp.where(flag, 1, 0).astype(jnp.int32)

    pl.semaphore_wait(barrier, 1 + one(has[0]) + one(has[1])
                      + one(last_core) * (one(next_cut) + one(prev_cut)))

    for side in range(2):
        @pl.when(has[side])
        def _():
            for which in range(2):
                given(side, which).start()

    for side, index in ((0, 0), (1, depth + 1)):
        @pl.when(jnp.logical_not(has[side]))
        def _():
            zero = jnp.zeros((nx, ny), jnp.float32)
            u0[index] = zero
            kap[index] = zero
            for i in range(5):
                for n in range(2):
                    its[i, n, index] = zero

    def bring(p, carry):
        for r in range(chunks):
            u0[p + 1, rows(r)] = u_ref[p, rows(r)]
            kap[p + 1, rows(r)] = k_ref[p, rows(r)]
        conduct(0, lambda i, q: u0[i, q], p + 1)
        return carry

    def inner(body):
        lax.fori_loop(1, top, lambda p, carry: (body(p), carry)[1], 0)

    lax.fori_loop(0, depth, bring, 0)
    inner(first)
    edges = ((0, 0, 0), (1, top, depth + 1))
    for side, p, index in edges:
        @pl.when(has[side])
        def _():
            for which in range(2):
                given(1 - side, which).wait_recv()
        conduct(0, lambda i, q: u0[i, q], index)
        first(p)

        @pl.when(has[side])
        def _():
            for n in range(2):
                halo(0, side, n).start()

    def sweep_step(i):
        for side, p, index in edges:
            for n in range(2):
                @pl.when(has[side])
                def _():
                    halo(i, 1 - side, n).wait_recv()
                jacobi(i, n, p)
                if i < 4:
                    @pl.when(has[side])
                    def _():
                        halo(i + 1, side, n).start()

        def body(p):
            for n in range(2):
                jacobi(i, n, p)
        inner(body)

    sweep_step(0)
    sweep_step(1)

    @pl.when(jnp.logical_and(last_core, next_cut))
    def _():
        for p in range(depth):
            ending(p).start()

    def both(body):
        lax.fori_loop(0, 2, lambda n, carry: (body(n), carry)[1], 0)

    def state_cond(p):
        for n in range(2):
            conduct(n, lambda i, q: its[2, n, i, q], p + 1)

    lax.fori_loop(0, depth, lambda p, carry: (state_cond(p), carry)[1], 0)

    def middle(p):
        def body(n):
            second(n, p)
            terms(n, p).start()
        both(body)
    inner(middle)
    for side, p, index in edges:
        @pl.when(has[side])
        def _():
            for n in range(2):
                halo(2, 1 - side, n).wait_recv()

        def body(n):
            conduct(n, lambda i, q: its[2, n, i, q], index)
            second(n, p)
            terms(n, p).start()
        both(body)

    @pl.when(jnp.logical_not(prev_cut))
    def _():
        def body(p, carry):
            beg[p] = u_ref[p]
            return carry
        lax.fori_loop(0, depth, body, 0)

    @pl.when(jnp.logical_and(prev_cut, last_core))
    def _():
        for p in range(depth):
            ending(p).wait_recv()
            forward(p).start()

    @pl.when(jnp.logical_and(prev_cut, jnp.logical_not(last_core)))
    def _():
        for p in range(depth):
            forward(p).wait_recv()

    def arrived(p):
        for n in range(2):
            terms(n, p).wait_recv()

    for side, p, index in edges:
        arrived(p)
        combine(p)

        @pl.when(has[side])
        def _():
            for n in range(2):
                halo(3, side, n).start()

    def rest(p):
        arrived(p)
        combine(p)
    inner(rest)
    sweep_step(3)
    sweep_step(4)

    for side in range(2):
        @pl.when(has[side])
        def _():
            for which in range(2):
                given(side, which).wait_send()
            for i in range(5):
                for n in range(2):
                    halo(i, side, n).wait_send()
    for n in range(2):
        for p in range(depth):
            terms(n, p).wait_send()

    @pl.when(jnp.logical_and(last_core, next_cut))
    def _():
        for p in range(depth):
            ending(p).wait_send()

    @pl.when(jnp.logical_and(last_core, prev_cut))
    def _():
        for p in range(depth):
            forward(p).wait_send()


def body(u_start, kappa, source):
    depth, nx, ny = u_start.shape
    f32 = jnp.float32
    peers, slices = lax.axis_size("space"), lax.axis_size("cuts")
    dma = pltpu.SemaphoreType.DMA

    def run(*refs):
        kernel(peers, slices, *refs)

    out = pl.pallas_call(
        run,
        out_shape=jax.ShapeDtypeStruct((2, depth, nx, ny), f32),
        in_specs=[pl.BlockSpec(memory_space=pltpu.VMEM)] * 3,
        out_specs=pl.BlockSpec(memory_space=pltpu.VMEM),
        scratch_shapes=[
            pltpu.VMEM((depth + 2, nx, ny), f32),
            pltpu.VMEM((depth + 2, nx, ny), f32),
            pltpu.VMEM((5, 2, depth + 2, nx, ny), f32),
            pltpu.VMEM((2, depth + 2, nx, ny), f32),
            pltpu.VMEM((2, 6, depth, nx, ny), f32),
            pltpu.VMEM((2, depth, nx, ny), f32),
            pltpu.VMEM((2, depth, nx, ny), f32),
            pltpu.VMEM((2, depth, nx, ny), f32),
            pltpu.VMEM((2, depth, nx, ny), f32),
            pltpu.VMEM((2, depth, nx, ny), f32),
            pltpu.VMEM((depth, nx, ny), f32),
            dma((2, 2)), dma((2, 2)),
            dma((5, 2, 2)), dma((5, 2, 2)),
            dma((2, depth)), dma((2, depth)),
            dma((depth,)), dma((depth,)),
            dma((depth,)), dma((depth,)),
        ],
        compiler_params=pltpu.CompilerParams(
            collective_id=0, has_side_effects=True, vmem_limit_bytes=40 * 1024 * 1024),
    )(u_start, kappa, source[0])
    return out[None]


def solution(mesh):
    placed = (
        P(("group", "space"), None, None),
        P("space", None, None),
        P("cuts", ("group", "space"), None, None),
    )
    return jax.shard_map(
        body,
        mesh=mesh,
        in_specs=placed,
        out_specs=P(("group", "cuts"), "node", "space", None, None),
        check_vma=False,
    )
```

profile of v0, /device:TPU:0, one launch (start us, length us, event | category | flops | bytes accessed | tf_op | source)
XLA Modules:
  0.0 49.2 jit_solution(11312130764560726230)
XLA Ops:
  0.0 0.0 copy-start
  0.0 1.0 %copy-done = f32[4,64,512]{2,1,0:T(8,128)S(1)} copy-done((f32[4,64,512]{2,1,0:T(8,128)S(1)}, f32[4,64,512]{2,1,0:T(8,128)}, u32[]{:S(2)}) %copy-start) | copy-done | bytes 524312
  1.0 0.0 copy-start.1
  1.0 1.0 %copy-done.1 = f32[4,64,512]{2,1,0:T(8,128)S(1)} copy-done((f32[4,64,512]{2,1,0:T(8,128)S(1)}, f32[4,64,512]{2,1,0:T(8,128)}, u32[]{:S(2)}) %copy-start.1) | copy-done | bytes 524312
  2.1 0.0 copy-start.2
  2.1 1.0 %copy-done.2 = f32[1,4,64,512]{3,2,1,0:T(8,128)S(1)} copy-done((f32[1,4,64,512]{3,2,1,0:T(8,128)S(1)}, f32[1,4,64,512]{3,2,1,0:T(8,128)}, u32[]{:S(2)}) %copy-start.2) | copy-done | bytes 524312
  3.1 45.1 %shard_map.37 = f32[2,4,64,512]{3,2,1,0:T(8,128)S(1)} custom-call(f32[4,64,512]{2,1,0:T(8,128)S(1)} %copy-done, f32[4,64,512]{2,1,0:T(8,128)S(1)} %copy-done.1, f32[4,64,512]{2,1,0:T(8,128)S(1)} %bitcast.3), custom_call_target="tpu_custom_call" | custom-call | tf_op jit(solution)/shard_map/pallas_call | solution.py:375
  48.3 1.0 %copy.5 = f32[1,2,4,64,512]{4,3,2,1,0:T(8,128)} copy(f32[1,2,4,64,512]{4,3,2,1,0:T(8,128)S(1)} %bitcast.2) | data formatting | bytes 2097152
Async XLA Ops:
  0.0 1.0 %copy-start = (f32[4,64,512]{2,1,0:T(8,128)S(1)}, f32[4,64,512]{2,1,0:T(8,128)}, u32[]{:S(2)}) copy-start(f32[4,64,512]{2,1,0:T(8,128)} %refs_0_.1) | copy-start | bytes 1572868
  1.0 1.0 %copy-start.1 = (f32[4,64,512]{2,1,0:T(8,128)S(1)}, f32[4,64,512]{2,1,0:T(8,128)}, u32[]{:S(2)}) copy-start(f32[4,64,512]{2,1,0:T(8,128)} %refs_1_.1) | copy-start | bytes 1572868
  2.1 1.0 %copy-start.2 = (f32[1,4,64,512]{3,2,1,0:T(8,128)S(1)}, f32[1,4,64,512]{3,2,1,0:T(8,128)}, u32[]{:S(2)}) copy-start(f32[1,4,64,512]{3,2,1,0:T(8,128)} %param.5) | copy-start | bytes 1572868
where the time goes:
time: 50.2 us; the launch traced here: 49.2 us
  Pallas kernels  45.1 us (90%)
  local copies, waits for them, and re-layouts  4.1 us (8%)
    pallas_call x1, Pallas kernels, body(): pl.pallas_call(run, out_shape=jax.ShapeDtypeStruct((2, depth, nx, ny), f3...  45.1 us
    unnamed x7, local copies, waits for them, and re-layouts  4.1 us

commit v1 on v0

v1 whole, which is shorter than its diff:
```python
import jax
import jax.numpy as jnp
import numpy as np
from jax import lax
from jax.experimental import pallas as pl
from jax.experimental.pallas import tpu as pltpu
from jax.sharding import PartitionSpec as P

DT = 0.5
MESH = pl.DeviceIdType.MESH
ROWS = 8
WIDE = 4
NEAR = 3


def radau_tables():
    nodes = [0.08858795951270396, 0.4094668644407347, 0.7876594617608471, 1.0]
    table = []
    for row_node in range(4):
        entries = []
        for basis in range(4):
            coeffs = [1.0]
            for other in range(4):
                if other == basis:
                    continue
                scale = 1.0 / (nodes[basis] - nodes[other])
                longer = [0.0] * (len(coeffs) + 1)
                for power in range(len(coeffs)):
                    longer[power + 1] += coeffs[power] * scale
                    longer[power] -= coeffs[power] * nodes[other] * scale
                coeffs = longer
            integral = 0.0
            for power in range(len(coeffs)):
                integral += coeffs[power] * nodes[row_node] ** (power + 1) / (power + 1)
            entries.append(integral)
        table.append(entries)
    return (np.array(table), np.array(nodes) / 4.0)


def kernel(peers, slices, u_ref, k_ref, s_ref, out_ref, kap, u0, srcs, its, cond, wts, base, oper, dinv, flx, far, beg,
           load_sem, in_send, in_recv, pass_send, pass_recv, halo_send, halo_recv, op_send, op_recv, cut_send, cut_recv, fwd_send, fwd_recv):
    depth, nx, ny = u_ref.shape
    top = depth - 1
    qnp, dnp = radau_tables()
    z, nd, cut = lax.axis_index("space"), lax.axis_index("node"), lax.axis_index("cuts")
    has = (z > 0, z < peers - 1)
    next_cut, prev_cut = cut < slices - 1, cut > 0
    last_core = nd == 1

    def pick(low, high):
        return jnp.where(nd == 0, jnp.float32(low), jnp.float32(high))

    step = [pick(DT * dnp[n], DT * dnp[n + 2]) for n in range(2)]
    whole = [pick(DT * qnp[n].sum(), DT * qnp[n + 2].sum()) for n in range(2)]
    own = [[pick(DT * qnp[n, j], DT * qnp[n + 2, j + 2]) for j in range(2)] for n in range(2)]
    away = [[pick(DT * qnp[n, j + 2], DT * qnp[n + 2, j]) for j in range(2)] for n in range(2)]

    row = lax.broadcasted_iota(jnp.int32, (ROWS, ny), 0)
    lane = lax.broadcasted_iota(jnp.int32, (ROWS, ny), 1)
    chunks = nx // ROWS

    def rows(r):
        return slice(r * ROWS, (r + 1) * ROWS)

    def sides(ref, r):
        here = ref(0, r)
        prev = ref(0, r - 1) if r > 0 else here
        succ = ref(0, r + 1) if r < chunks - 1 else here
        return [
            ref(1, r), ref(-1, r),
            pltpu.roll(jnp.where(row == 0, succ, here), ROWS - 1, 0),
            pltpu.roll(jnp.where(row == ROWS - 1, prev, here), 1, 0),
            pltpu.roll(here, ny - 1, 1),
            pltpu.roll(here, 1, 1),
        ]

    def inside(parts, r):
        out = list(parts)
        if r == chunks - 1:
            out[2] = jnp.where(row == ROWS - 1, 0.0, out[2])
        if r == 0:
            out[3] = jnp.where(row == 0, 0.0, out[3])
        out[4] = jnp.where(lane == ny - 1, 0.0, out[4])
        out[5] = jnp.where(lane == 0, 0.0, out[5])
        return out

    def stencil(n, field, p, r):
        half = cond[n, p + WIDE, rows(r)]
        near = inside(sides(lambda d, q: cond[n, p + WIDE + d, rows(q)], r), r)
        w = [half + c for c in near]
        diag = (w[0] + w[1]) + (w[2] + w[3]) + (w[4] + w[5])
        w = inside(w, r)
        v = sides(lambda d, q: field(p + d, rows(q)), r)
        flow = (w[0] * v[0] + w[1] * v[1]) + (w[2] * v[2] + w[3] * v[3]) + (w[4] * v[4] + w[5] * v[5])
        return w, diag, flow

    def start_field(p, q):
        return u0[p + WIDE, q]

    def later_field(n):
        return lambda p, q: its[2, n, p + NEAR, q]

    def conduct(n, field, p):
        for r in range(chunks):
            v = field(p, rows(r))
            cond[n, p + WIDE, rows(r)] = 0.5 * kap[p + WIDE, rows(r)] * (1.0 + v * v)

    def first(p):
        for r in range(chunks):
            w, diag, flow = stencil(0, start_field, p, r)
            v = u0[p + WIDE, rows(r)]
            op = flow - diag * v
            slope = op + srcs[p + WIDE, rows(r)]
            for n in range(2):
                inv = 1.0 / (1.0 + step[n] * diag)
                t = inv * (v + whole[n] * slope - step[n] * op)
                base[n, p + NEAR, rows(r)] = t
                scale = step[n] * inv
                for k in range(6):
                    wts[n, k, p + NEAR, rows(r)] = w[k] * scale
                its[0, n, p + NEAR, rows(r)] = t + scale * flow

    def second(n, p):
        s = jnp.where(n == 0, step[0], step[1])
        for r in range(chunks):
            w, diag, flow = stencil(n, later_field(n), p, r)
            oper[n, p, rows(r)] = flow - diag * its[2, n, p + NEAR, rows(r)]
            inv = 1.0 / (1.0 + s * diag)
            scale = s * inv
            for k in range(6):
                wts[n, k, p + NEAR, rows(r)] = w[k] * scale
            dinv[n, p, rows(r)] = inv
            flx[n, p, rows(r)] = scale * flow

    def combine(p):
        for r in range(chunks):
            q = rows(r)
            a, b, c, d = oper[0, p, q], oper[1, p, q], far[0, p, q], far[1, p, q]
            start, src = beg[p, q], srcs[p + WIDE, q]
            for n in range(2):
                t = start + own[n][0] * a + own[n][1] * b + away[n][0] * c + away[n][1] * d + whole[n] * src
                t = dinv[n, p, q] * (t - step[n] * (a, b)[n])
                base[n, p + NEAR, q] = t
                its[3, n, p + NEAR, q] = t + flx[n, p, q]

    def jacobi(i, n, p):
        for r in range(chunks):
            v = sides(lambda d, q: its[i, n, p + NEAR + d, rows(q)], r)
            w = [wts[n, k, p + NEAR, rows(r)] for k in range(6)]
            got = base[n, p + NEAR, rows(r)] + (w[0] * v[0] + w[1] * v[1])
            got = got + ((w[2] * v[2] + w[3] * v[3]) + (w[4] * v[4] + w[5] * v[5]))
            if i == 4:
                out_ref[n, p, rows(r)] = got
            else:
                its[i + 1, n, p + NEAR, rows(r)] = got

    def halo(i, side, n):
        return pltpu.make_async_remote_copy(
            src_ref=its.at[i, n, NEAR if side == 0 else top + NEAR],
            dst_ref=its.at[i, n, depth + NEAR if side == 0 else NEAR - 1],
            send_sem=halo_send.at[i - 3, side, n], recv_sem=halo_recv.at[i - 3, side, n],
            device_id={"space": z - 1 if side == 0 else z + 1}, device_id_type=MESH)

    given_refs = ((u_ref, u0), (k_ref, kap), (s_ref, srcs))
    items = [(d, which) for d in range(1, WIDE + 1) for which in range(3 if d < WIDE else 2)]
    place = {item: slot for slot, item in enumerate(items)}

    def beyond(side, d):
        return -d if side == 0 else top + d

    def given(side, item):
        d, which = item
        src, dst = given_refs[which]
        return pltpu.make_async_remote_copy(
            src_ref=src.at[d - 1 if side == 0 else depth - d],
            dst_ref=dst.at[beyond(1 - side, d) + WIDE],
            send_sem=in_send.at[side, place[item]], recv_sem=in_recv.at[side, place[item]],
            device_id={"space": z - 1 if side == 0 else z + 1}, device_id_type=MESH)

    def passed(side, item):
        d, which = item
        ref = given_refs[which][1].at[beyond(side, d) + WIDE]
        return pltpu.make_async_remote_copy(
            src_ref=ref, dst_ref=ref,
            send_sem=pass_send.at[side, place[item]], recv_sem=pass_recv.at[side, place[item]],
            device_id={"node": 1 - nd}, device_id_type=MESH)

    def load(which):
        src, dst = given_refs[which]
        return pltpu.make_async_copy(src, dst.at[pl.ds(WIDE, depth)], load_sem.at[which])

    def terms(n, p):
        return pltpu.make_async_remote_copy(
            src_ref=oper.at[n, p], dst_ref=far.at[n, p],
            send_sem=op_send.at[n, p], recv_sem=op_recv.at[n, p],
            device_id={"node": 1 - nd}, device_id_type=MESH)

    def ending(p):
        return pltpu.make_async_remote_copy(
            src_ref=its.at[2, 1, p + NEAR], dst_ref=beg.at[p],
            send_sem=cut_send.at[p], recv_sem=cut_recv.at[p],
            device_id={"cuts": cut + 1}, device_id_type=MESH)

    def forward(p):
        return pltpu.make_async_remote_copy(
            src_ref=beg.at[p], dst_ref=beg.at[p],
            send_sem=fwd_send.at[p], recv_sem=fwd_recv.at[p],
            device_id={"node": 1 - nd}, device_id_type=MESH)

    for which in range(3):
        load(which).start()
    barrier = pltpu.get_barrier_semaphore()

    def greet(**where):
        pl.semaphore_signal(barrier, inc=1, device_id=where, device_id_type=MESH)

    @pl.when(has[0])
    def _():
        greet(space=z - 1)

    @pl.when(has[1])
    def _():
        greet(space=z + 1)

    greet(node=1 - nd)

    @pl.when(jnp.logical_and(last_core, next_cut))
    def _():
        greet(cuts=cut + 1)

    @pl.when(jnp.logical_and(last_core, prev_cut))
    def _():
        greet(cuts=cut - 1)

    def one(flag):
        return jnp.where(flag, 1, 0).astype(jnp.int32)

    pl.semaphore_wait(barrier, 1 + one(has[0]) + one(has[1])
                      + one(last_core) * (one(next_cut) + one(prev_cut)))

    for core in range(2):
        @pl.when(nd == core)
        def _():
            for side in range(2):
                @pl.when(has[side])
                def _():
                    for item in items:
                        if place[item] % 2 == core:
                            given(side, item).start()

    for side in range(2):
        @pl.when(jnp.logical_not(has[side]))
        def _():
            zero = jnp.zeros((nx, ny), jnp.float32)
            p = beyond(side, 1)
            u0[p + WIDE] = zero
            for n in range(2):
                cond[n, p + WIDE] = zero
                for i in range(5):
                    its[i, n, p + NEAR] = zero

    def each(low, high, body):
        lax.fori_loop(low, high, lambda p, carry: (body(p), carry)[1], 0)

    def inner(body):
        each(1, top, body)

    load(0).wait()
    load(1).wait()
    each(0, depth, lambda p: conduct(0, start_field, p))
    load(2).wait()
    inner(first)

    def fetch(d):
        for core in range(2):
            @pl.when(nd == core)
            def _():
                for mine in (True, False):
                    for side in range(2):
                        @pl.when(has[side])
                        def _():
                            for item in items:
                                if item[0] == d and (place[item] % 2 == core) == mine:
                                    if mine:
                                        given(1 - side, item).wait_recv()
                                        passed(side, item).start()
                                    else:
                                        passed(side, item).wait_recv()

    def both_sides(d, body):
        for side in range(2):
            if d > 0:
                @pl.when(has[side])
                def _():
                    body(beyond(side, d))
            else:
                body(beyond(side, d))

    def iterate(i, d):
        def planes(p):
            for n in range(2):
                jacobi(i, n, p)
        if d < 0:
            inner(planes)
        else:
            both_sides(d, planes)

    def stage(d):
        fetch(d)
        both_sides(d, lambda p: conduct(0, start_field, p))
        both_sides(d - 1, first)
        iterate(0, d - 2)
        if d > 1:
            iterate(1, d - 3)

    for d in range(1, WIDE):
        stage(d)

    @pl.when(jnp.logical_and(last_core, next_cut))
    def _():
        for p in range(depth):
            ending(p).start()

    def both(body):
        each(0, 2, body)

    def middle(p):
        def body(n):
            second(n, p)
            terms(n, p).start()
        both(body)

    def state_cond(p):
        for n in range(2):
            conduct(n, later_field(n), p)

    each(0, depth, state_cond)
    inner(middle)
    stage(WIDE)

    edges = ((0, 0), (1, top))
    for side, p in edges:
        @pl.when(has[side])
        def _():
            state_cond(beyond(side, 1))
        middle(p)

    def sweep_step(i):
        for side, p in edges:
            for n in range(2):
                @pl.when(has[side])
                def _():
                    halo(i, 1 - side, n).wait_recv()
                jacobi(i, n, p)
                if i < 4:
                    @pl.when(has[side])
                    def _():
                        halo(i + 1, side, n).start()

        def body(p):
            for n in range(2):
                jacobi(i, n, p)
        inner(body)

    @pl.when(jnp.logical_not(prev_cut))
    def _():
        def body(p, carry):
            beg[p] = u0[p + WIDE]
            return carry
        lax.fori_loop(0, depth, body, 0)

    @pl.when(jnp.logical_and(prev_cut, last_core))
    def _():
        for p in range(depth):
            ending(p).wait_recv()
            forward(p).start()

    @pl.when(jnp.logical_and(prev_cut, jnp.logical_not(last_core)))
    def _():
        for p in range(depth):
            forward(p).wait_recv()

    def arrived(p):
        for n in range(2):
            terms(n, p).wait_recv()

    for side, p in edges:
        arrived(p)
        combine(p)

        @pl.when(has[side])
        def _():
            for n in range(2):
                halo(3, side, n).start()

    def rest(p):
        arrived(p)
        combine(p)
    inner(rest)
    sweep_step(3)
    sweep_step(4)

    for side in range(2):
        @pl.when(has[side])
        def _():
            for i in range(3, 5):
                for n in range(2):
                    halo(i, side, n).wait_send()
    for core in range(2):
        @pl.when(nd == core)
        def _():
            for side in range(2):
                @pl.when(has[side])
                def _():
                    for item in items:
                        if place[item] % 2 == core:
                            given(side, item).wait_send()
                            passed(side, item).wait_send()
    for n in range(2):
        for p in range(depth):
            terms(n, p).wait_send()

    @pl.when(jnp.logical_and(last_core, next_cut))
    def _():
        for p in range(depth):
            ending(p).wait_send()

    @pl.when(jnp.logical_and(last_core, prev_cut))
    def _():
        for p in range(depth):
            forward(p).wait_send()


def body(u_start, kappa, source):
    depth, nx, ny = u_start.shape
    f32 = jnp.float32
    peers, slices = lax.axis_size("space"), lax.axis_size("cuts")
    dma = pltpu.SemaphoreType.DMA

    def run(*refs):
        kernel(peers, slices, *refs)

    out = pl.pallas_call(
        run,
        out_shape=jax.ShapeDtypeStruct((2, depth, nx, ny), f32),
        in_specs=[pl.BlockSpec(memory_space=pltpu.HBM)] * 3,
        out_specs=pl.BlockSpec(memory_space=pltpu.VMEM),
        scratch_shapes=[
            pltpu.VMEM((depth + 2 * WIDE, nx, ny), f32),
            pltpu.VMEM((depth + 2 * WIDE, nx, ny), f32),
            pltpu.VMEM((depth + 2 * WIDE, nx, ny), f32),
            pltpu.VMEM((5, 2, depth + 2 * NEAR, nx, ny), f32),
            pltpu.VMEM((2, depth + 2 * WIDE, nx, ny), f32),
            pltpu.VMEM((2, 6, depth + 2 * NEAR, nx, ny), f32),
            pltpu.VMEM((2, depth + 2 * NEAR, nx, ny), f32),
            pltpu.VMEM((2, depth, nx, ny), f32),
            pltpu.VMEM((2, depth, nx, ny), f32),
            pltpu.VMEM((2, depth, nx, ny), f32),
            pltpu.VMEM((2, depth, nx, ny), f32),
            pltpu.VMEM((depth, nx, ny), f32),
            dma((3,)), dma((2, 11)), dma((2, 11)), dma((2, 11)), dma((2, 11)),
            dma((2, 2, 2)), dma((2, 2, 2)),
            dma((2, depth)), dma((2, depth)),
            dma((depth,)), dma((depth,)),
            dma((depth,)), dma((depth,)),
        ],
        compiler_params=pltpu.CompilerParams(
            collective_id=0, has_side_effects=True, vmem_limit_bytes=52 * 1024 * 1024),
    )(u_start, kappa, source[0])
    return out[None]


def solution(mesh):
    placed = (
        P(("group", "space"), None, None),
        P("space", None, None),
        P("cuts", ("group", "space"), None, None),
    )
    return jax.shard_map(
        body,
        mesh=mesh,
        in_specs=placed,
        out_specs=P(("group", "cuts"), "node", "space", None, None),
        check_vma=False,
    )
```

time: 50.2 us -> 50.4 us (level); the launches traced: 49.2 us -> 50.1 us
  local copies, waits for them, and re-layouts: 4.1 us -> 5.39 us
    unnamed x7, local copies, waits for them, and re-layouts: 4.1 us -> 5.39 us
where the time goes in v1:
time: 50.4 us; the launch traced here: 50.1 us
  Pallas kernels  44.7 us (89%)
  local copies, waits for them, and re-layouts  5.39 us (11%)
    pallas_call x1, Pallas kernels, body(): pl.pallas_call(run, out_shape=jax.ShapeDtypeStruct((2, depth, nx, ny), f3...  44.7 us
    unnamed x7, local copies, waits for them, and re-layouts  5.39 us

profile of v1, /device:TPU:0, one launch (start us, length us, event | category | flops | bytes accessed | tf_op | source)
XLA Modules:
  0.0 50.1 jit_solution(3081585462175912127)
XLA Ops:
  0.0 0.0 copy-start
  0.0 1.0 %copy-done = f32[4,64,512]{2,1,0:T(8,128)S(1)} copy-done((f32[4,64,512]{2,1,0:T(8,128)S(1)}, f32[4,64,512]{2,1,0:T(8,128)}, u32[]{:S(2)}) %copy-start) | copy-done | bytes 524312
  1.0 0.0 copy-start.1
  1.0 1.0 %copy-done.1 = f32[4,64,512]{2,1,0:T(8,128)S(1)} copy-done((f32[4,64,512]{2,1,0:T(8,128)S(1)}, f32[4,64,512]{2,1,0:T(8,128)}, u32[]{:S(2)}) %copy-start.1) | copy-done | bytes 524312
  2.1 0.0 copy-start.2
  2.1 1.0 %copy-done.2 = f32[1,4,64,512]{3,2,1,0:T(8,128)S(1)} copy-done((f32[1,4,64,512]{3,2,1,0:T(8,128)S(1)}, f32[1,4,64,512]{3,2,1,0:T(8,128)}, u32[]{:S(2)}) %copy-start.2) | copy-done | bytes 524312
  3.1 44.7 %shard_map.37 = f32[2,4,64,512]{3,2,1,0:T(8,128)} custom-call(f32[4,64,512]{2,1,0:T(8,128)S(1)} %copy-done, f32[4,64,512]{2,1,0:T(8,128)S(1)} %copy-done.1, f32[4,64,512]{2,1,0:T(8,128)S(1)} %bitcast.2), custom_call_target="tpu_custom_call" | custom-call | tf_op jit(solution)/shard_map/pallas_call | solution.py:443
  47.8 2.3 %copy.5 = f32[1,2,4,64,512]{4,3,2,1,0:T(8,128)} copy(f32[1,2,4,64,512]{4,3,2,1,0:T(8,128)} %bitcast.3) | data formatting | bytes 2097152
Async XLA Ops:
  0.0 1.0 %copy-start = (f32[4,64,512]{2,1,0:T(8,128)S(1)}, f32[4,64,512]{2,1,0:T(8,128)}, u32[]{:S(2)}) copy-start(f32[4,64,512]{2,1,0:T(8,128)} %refs_0_.1) | copy-start | bytes 1572868
  1.0 1.0 %copy-start.1 = (f32[4,64,512]{2,1,0:T(8,128)S(1)}, f32[4,64,512]{2,1,0:T(8,128)}, u32[]{:S(2)}) copy-start(f32[4,64,512]{2,1,0:T(8,128)} %refs_1_.1) | copy-start | bytes 1572868
  2.1 1.0 %copy-start.2 = (f32[1,4,64,512]{3,2,1,0:T(8,128)S(1)}, f32[1,4,64,512]{3,2,1,0:T(8,128)}, u32[]{:S(2)}) copy-start(f32[1,4,64,512]{3,2,1,0:T(8,128)} %param.5) | copy-start | bytes 1572868

commit v2 on v1

--- a/solution.py
+++ b/solution.py
@@ -313,13 +313,31 @@
         if d > 1:
             iterate(1, d - 3)
 
-    for d in range(1, WIDE):
-        stage(d)
-
-    @pl.when(jnp.logical_and(last_core, next_cut))
-    def _():
-        for p in range(depth):
-            ending(p).start()
+    within = tuple(range(1, top))
+
+    def hand_over(planes):
+        @pl.when(jnp.logical_and(last_core, next_cut))
+        def _():
+            for p in planes:
+                ending(p).start()
+
+    def take_over(planes):
+        @pl.when(jnp.logical_and(last_core, prev_cut))
+        def _():
+            for p in planes:
+                ending(p).wait_recv()
+                forward(p).start()
+
+    def begun(p):
+        @pl.when(jnp.logical_and(prev_cut, jnp.logical_not(last_core)))
+        def _():
+            forward(p).wait_recv()
+
+    stage(1)
+    stage(2)
+    hand_over(within)
+    stage(3)
+    hand_over((0, top))
 
     def both(body):
         each(0, 2, body)
@@ -336,7 +354,9 @@
 
     each(0, depth, state_cond)
     inner(middle)
+    take_over(within)
     stage(WIDE)
+    take_over((0, top))
 
     edges = ((0, 0), (1, top))
     for side, p in edges:
@@ -346,8 +366,8 @@
         middle(p)
 
     def sweep_step(i):
-        for side, p in edges:
-            for n in range(2):
+        for n in range(2):
+            for side, p in edges:
                 @pl.when(has[side])
                 def _():
                     halo(i, 1 - side, n).wait_recv()
@@ -369,22 +389,12 @@
             return carry
         lax.fori_loop(0, depth, body, 0)
 
-    @pl.when(jnp.logical_and(prev_cut, last_core))
-    def _():
-        for p in range(depth):
-            ending(p).wait_recv()
-            forward(p).start()
-
-    @pl.when(jnp.logical_and(prev_cut, jnp.logical_not(last_core)))
-    def _():
-        for p in range(depth):
-            forward(p).wait_recv()
-
     def arrived(p):
         for n in range(2):
             terms(n, p).wait_recv()
 
     for side, p in edges:
+        begun(p)
         arrived(p)
         combine(p)
 
@@ -394,6 +404,7 @@
                 halo(3, side, n).start()
 
     def rest(p):
+        begun(p)
         arrived(p)
         combine(p)
     inner(rest)

time: 50.4 us -> 50.3 us (level)
  no operation moved by 1% of the time
where the time goes in v2:
time: 50.3 us; the launch traced here: 50 us
  Pallas kernels  44.6 us (89%)
  local copies, waits for them, and re-layouts  5.39 us (11%)
    pallas_call x1, Pallas kernels, body(): pl.pallas_call(run, out_shape=jax.ShapeDtypeStruct((2, depth, nx, ny), f3...  44.6 us
    unnamed x7, local copies, waits for them, and re-layouts  5.39 us

profile of v2, /device:TPU:0, one launch (start us, length us, event | category | flops | bytes accessed | tf_op | source)
XLA Modules:
  0.0 50.0 jit_solution(8155484199335589246)
XLA Ops:
  0.0 0.0 copy-start
  0.0 1.0 %copy-done = f32[4,64,512]{2,1,0:T(8,128)S(1)} copy-done((f32[4,64,512]{2,1,0:T(8,128)S(1)}, f32[4,64,512]{2,1,0:T(8,128)}, u32[]{:S(2)}) %copy-start) | copy-done | bytes 524312
  1.0 0.0 copy-start.1
  1.0 1.0 %copy-done.1 = f32[4,64,512]{2,1,0:T(8,128)S(1)} copy-done((f32[4,64,512]{2,1,0:T(8,128)S(1)}, f32[4,64,512]{2,1,0:T(8,128)}, u32[]{:S(2)}) %copy-start.1) | copy-done | bytes 524312
  2.1 0.0 copy-start.2
  2.1 1.0 %copy-done.2 = f32[1,4,64,512]{3,2,1,0:T(8,128)S(1)} copy-done((f32[1,4,64,512]{3,2,1,0:T(8,128)S(1)}, f32[1,4,64,512]{3,2,1,0:T(8,128)}, u32[]{:S(2)}) %copy-start.2) | copy-done | bytes 524312
  3.1 44.6 %shard_map.37 = f32[2,4,64,512]{3,2,1,0:T(8,128)} custom-call(f32[4,64,512]{2,1,0:T(8,128)S(1)} %copy-done, f32[4,64,512]{2,1,0:T(8,128)S(1)} %copy-done.1, f32[4,64,512]{2,1,0:T(8,128)S(1)} %bitcast.2), custom_call_target="tpu_custom_call" | custom-call | tf_op jit(solution)/shard_map/pallas_call | solution.py:454
  47.7 2.3 %copy.5 = f32[1,2,4,64,512]{4,3,2,1,0:T(8,128)} copy(f32[1,2,4,64,512]{4,3,2,1,0:T(8,128)} %bitcast.3) | data formatting | bytes 2097152
Async XLA Ops:
  0.0 1.0 %copy-start = (f32[4,64,512]{2,1,0:T(8,128)S(1)}, f32[4,64,512]{2,1,0:T(8,128)}, u32[]{:S(2)}) copy-start(f32[4,64,512]{2,1,0:T(8,128)} %refs_0_.1) | copy-start | bytes 1572868
  1.0 1.0 %copy-start.1 = (f32[4,64,512]{2,1,0:T(8,128)S(1)}, f32[4,64,512]{2,1,0:T(8,128)}, u32[]{:S(2)}) copy-start(f32[4,64,512]{2,1,0:T(8,128)} %refs_1_.1) | copy-start | bytes 1572868
  2.1 1.0 %copy-start.2 = (f32[1,4,64,512]{3,2,1,0:T(8,128)S(1)}, f32[1,4,64,512]{3,2,1,0:T(8,128)}, u32[]{:S(2)}) copy-start(f32[1,4,64,512]{3,2,1,0:T(8,128)} %param.5) | copy-start | bytes 1572868

commit v3 on v0

--- a/solution.py
+++ b/solution.py
@@ -251,8 +251,8 @@
                 halo(0, side, n).start()
 
     def sweep_step(i):
-        for side, p, index in edges:
-            for n in range(2):
+        for n in range(2):
+            for side, p, index in edges:
                 @pl.when(has[side])
                 def _():
                     halo(i, 1 - side, n).wait_recv()

time: 50.2 us -> 49.5 us (0.986); the launches traced: 49.2 us -> 49.2 us
  no operation moved by 1% of the time
where the time goes in v3:
time: 49.5 us; the launch traced here: 49.2 us
  Pallas kernels  45.1 us (91%)
  local copies, waits for them, and re-layouts  4.1 us (8%)
    pallas_call x1, Pallas kernels, body(): pl.pallas_call(run, out_shape=jax.ShapeDtypeStruct((2, depth, nx, ny), f3...  45.1 us
    unnamed x7, local copies, waits for them, and re-layouts  4.1 us

profile of v3, /device:TPU:0, one launch (start us, length us, event | category | flops | bytes accessed | tf_op | source)
XLA Modules:
  0.0 49.2 jit_solution(17658737946623393555)
XLA Ops:
  0.0 0.0 copy-start
  0.0 1.0 %copy-done = f32[4,64,512]{2,1,0:T(8,128)S(1)} copy-done((f32[4,64,512]{2,1,0:T(8,128)S(1)}, f32[4,64,512]{2,1,0:T(8,128)}, u32[]{:S(2)}) %copy-start) | copy-done | bytes 524312
  1.0 0.0 copy-start.1
  1.0 1.0 %copy-done.1 = f32[4,64,512]{2,1,0:T(8,128)S(1)} copy-done((f32[4,64,512]{2,1,0:T(8,128)S(1)}, f32[4,64,512]{2,1,0:T(8,128)}, u32[]{:S(2)}) %copy-start.1) | copy-done | bytes 524312
  2.1 0.0 copy-start.2
  2.1 1.0 %copy-done.2 = f32[1,4,64,512]{3,2,1,0:T(8,128)S(1)} copy-done((f32[1,4,64,512]{3,2,1,0:T(8,128)S(1)}, f32[1,4,64,512]{3,2,1,0:T(8,128)}, u32[]{:S(2)}) %copy-start.2) | copy-done | bytes 524312
  3.1 45.1 %shard_map.37 = f32[2,4,64,512]{3,2,1,0:T(8,128)S(1)} custom-call(f32[4,64,512]{2,1,0:T(8,128)S(1)} %copy-done, f32[4,64,512]{2,1,0:T(8,128)S(1)} %copy-done.1, f32[4,64,512]{2,1,0:T(8,128)S(1)} %bitcast.3), custom_call_target="tpu_custom_call" | custom-call | tf_op jit(solution)/shard_map/pallas_call | solution.py:375
  48.3 1.0 %copy.5 = f32[1,2,4,64,512]{4,3,2,1,0:T(8,128)} copy(f32[1,2,4,64,512]{4,3,2,1,0:T(8,128)S(1)} %bitcast.2) | data formatting | bytes 2097152
Async XLA Ops:
  0.0 1.0 %copy-start = (f32[4,64,512]{2,1,0:T(8,128)S(1)}, f32[4,64,512]{2,1,0:T(8,128)}, u32[]{:S(2)}) copy-start(f32[4,64,512]{2,1,0:T(8,128)} %refs_0_.1) | copy-start | bytes 1572868
  1.0 1.0 %copy-start.1 = (f32[4,64,512]{2,1,0:T(8,128)S(1)}, f32[4,64,512]{2,1,0:T(8,128)}, u32[]{:S(2)}) copy-start(f32[4,64,512]{2,1,0:T(8,128)} %refs_1_.1) | copy-start | bytes 1572868
  2.1 1.0 %copy-start.2 = (f32[1,4,64,512]{3,2,1,0:T(8,128)S(1)}, f32[1,4,64,512]{3,2,1,0:T(8,128)}, u32[]{:S(2)}) copy-start(f32[1,4,64,512]{3,2,1,0:T(8,128)} %param.5) | copy-start | bytes 1572868
